TPU v7x, 32 devices: a whole 2x2x4 slice. The times are simulated.
32 devices in a mesh: rep: 2 (over y), wide: 2 (over core), narrow: 8 (over z, x).
Axes of the slice: x: 2, y: 2, z: 4, core: 2. Of those that a mesh axis runs over, the one named last changes fastest.
Arguments:
- queries: bfloat16 [8, 120, 4096], P(('rep', 'wide'), None, 'narrow'), parts along dimension 0, may hold values from -6 to 6
- layer_rows: bfloat16 [8, 120, 4096], P(('rep', 'wide'), None, 'narrow'), parts along dimension 0, may hold values from -6 to 6
- positions: int32 [8, 120], P(('rep', 'wide')), parts along dimension 0, may hold values from 0 to 2047, as said below
- counts: int32 [8], P('rep'), parts along dimension 0, may hold values from 1 to 120, 300 in all
- key_cache: bfloat16 [8, 65536, 128], P(('rep', 'wide'), 'narrow'), parts along dimension 0, may hold values from -400 to 400
- value_cache: bfloat16 [8, 65536, 128], P(('rep', 'wide'), 'narrow'), parts along dimension 0, may hold values from -6 to 6
- out_weight: bfloat16 [4096, 4096], P(None, 'narrow'), may hold values from -0.09375 to 0.09375
- ffn_gain: bfloat16 [4096], replicated, may hold values from 0.5 to 2
- w_gate: bfloat16 [12288, 4096], P('narrow'), may hold values from -0.09375 to 0.09375
- w_up: bfloat16 [12288, 4096], P('narrow'), may hold values from -0.09375 to 0.09375
- w_down: bfloat16 [4096, 12288], P('narrow'), may hold values from -0.0546875 to 0.0546875
Outputs:
- refreshed: bfloat16 [600, 4096], P(('rep', 'wide'), 'narrow'), parts along dimension 0
There are 2 independent parts, one for each index of `rep`. A program takes and returns all parts, laid end to end along the dimension named above; an argument that names none is the same for every part. Nothing has to cross between parts.
Inputs may be any that keep to these rules, and one draw needn't show every extreme that they name: Within each canvas the 120 slot positions are distinct. The live slots of a canvas are its first counts slots. The counts are taken part by part: the 4 counts of each part sum to 150 times the number of wide groups, so an array that holds several parts sums to that once for each part.
All inputs are finite; a program needn't handle non-finite values.
Results may differ from a plain program's by a relative error of at most 0.012.
The roundings to bfloat16 on the way count: a program that leaves them out, or rounds other values in their place, can miss the bound.
Values may be sent and summed in bfloat16 or wider, within the bound.
A program may use at most 128 MiB of HBM per device.

v0:
```python
import jax
import jax.numpy as jnp
from jax import lax
from jax.sharding import PartitionSpec as P

D = 4096
HEAD = 128
BAL = 150


epsilon = 1e-05


def from_partner(x, axis, distance):
    return lax.ppermute(x, axis, [(i, i ^ 1 << distance) for i in range(lax.axis_size(axis))])


def rotate_queries(queries_f32, positions):
    half_size = HEAD // 2
    frequency = 500000.0 ** (-2.0 * jnp.arange(half_size, dtype=jnp.float32) / HEAD)
    angles = positions.astype(jnp.float32)[..., None] * frequency
    cosine_table = jnp.cos(angles)[..., None, :]
    sine_table = jnp.sin(angles)[..., None, :]
    lower_half = queries_f32[..., :half_size]
    upper_half = queries_f32[..., half_size:]
    return jnp.concatenate(
        [
            lower_half * cosine_table - upper_half * sine_table,
            upper_half * cosine_table + lower_half * sine_table,
        ],
        axis=-1,
    )


def balanced_slots(counts, canvases, slot_cap, groups, share):
    canvas_total = counts.shape[0]
    canvas_end = jnp.cumsum(counts, dtype=jnp.int32)
    canvas_start = canvas_end - counts
    global_slot = jnp.arange(groups * share, dtype=jnp.int32)
    canvas_of = jnp.sum(
        (canvas_end[None, :] <= global_slot[:, None]).astype(jnp.int32), axis=1, dtype=jnp.int32
    )
    canvas_of = jnp.minimum(canvas_of, canvas_total - 1)
    matches = canvas_of[:, None] == jnp.arange(canvas_total, dtype=jnp.int32)[None, :]
    picked_start = jnp.sum(jnp.where(matches, canvas_start[None, :], 0), axis=1, dtype=jnp.int32)
    within = global_slot - picked_start
    source = canvas_of // canvases
    local_slot = canvas_of % canvases * slot_cap + within
    return (source.reshape(groups, share), local_slot.reshape(groups, share))


def route_rows(rows_local, counts, canvases, slot_cap, groups, share):
    source, local_slot = balanced_slots(counts, canvases, slot_cap, groups, share)
    from_here = source == lax.axis_index("wide")
    picked = jnp.take(rows_local, jnp.where(from_here, local_slot, 0).reshape(-1), axis=0)
    picked = picked.reshape(groups, share, rows_local.shape[1])
    return jnp.where(from_here[:, :, None], picked, jnp.zeros_like(picked))


def feed_forward(residual, ffn_gain, w_gate, w_up, w_down):
    gathered = lax.all_gather(residual, "narrow", axis=1, tiled=True).astype(jnp.float32)
    normed = (
        gathered
        * lax.rsqrt(jnp.mean(gathered * gathered, axis=1, keepdims=True) + epsilon)
        * ffn_gain.astype(jnp.float32)
    ).astype(jnp.bfloat16)
    contract = (((1,), (1,)), ((), ()))
    gate_sum = lax.dot_general(normed, w_gate, contract, preferred_element_type=jnp.float32)
    up_sum = lax.dot_general(normed, w_up, contract, preferred_element_type=jnp.float32)
    activated = (jax.nn.silu(gate_sum) * up_sum).astype(jnp.bfloat16)
    output = lax.dot_general(
        lax.all_gather(activated, "narrow", axis=1, tiled=True),
        w_down,
        contract,
        preferred_element_type=jnp.float32,
    )
    return (residual.astype(jnp.float32) + output).astype(jnp.bfloat16)


def per_device(
    queries,
    layer_rows,
    positions,
    counts,
    key_cache,
    value_cache,
    out_weight,
    ffn_gain,
    w_gate,
    w_up,
    w_down,
):
    canvases, slot_cap, feature_share = queries.shape
    head_count = D // HEAD
    narrow_count = lax.axis_size("narrow")
    groups = lax.axis_size("wide")
    row_count = canvases * slot_cap
    group_size = max(1, narrow_count // head_count)
    local_heads = max(1, head_count // narrow_count)
    bit_steps = group_size.bit_length() - 1
    device_index = lax.axis_index("narrow")
    joined = queries
    for level in range(bit_steps):
        partner = from_partner(joined, "narrow", level)
        upper_bit = device_index // 2**level % 2 == 1
        joined = jnp.where(
            upper_bit,
            jnp.concatenate([partner, joined], axis=2),
            jnp.concatenate([joined, partner], axis=2),
        )
    rotated = rotate_queries(
        joined.astype(jnp.float32).reshape(canvases, slot_cap, local_heads, HEAD), positions
    ).astype(jnp.bfloat16)
    block_rows = key_cache.shape[1] // local_heads
    key_blocks = key_cache.reshape(canvases, local_heads, block_rows, HEAD)
    value_blocks = value_cache.reshape(canvases, local_heads, block_rows, HEAD)
    scores = jnp.einsum(
        "crhd,chpd->chrp", rotated, key_blocks, preferred_element_type=jnp.float32
    ) * HEAD ** (-0.5)
    row_peak = jnp.max(scores, axis=3)
    for level in range(bit_steps):
        other_peak = from_partner(row_peak, "narrow", level)
        row_peak = jnp.maximum(row_peak, other_peak)
    exponent = jnp.exp(scores - row_peak[..., None])
    totals = jnp.sum(exponent, axis=3)
    mixture = jnp.einsum(
        "chrp,chpd->crhd",
        exponent.astype(jnp.bfloat16),
        value_blocks,
        preferred_element_type=jnp.float32,
    ).reshape(row_count, local_heads * HEAD)
    for level in reversed(range(bit_steps)):
        half_width = mixture.shape[1] // 2
        lower_part = mixture[:, :half_width]
        upper_part = mixture[:, half_width:]
        upper_bit = device_index // 2**level % 2 == 1
        outgoing = jnp.where(upper_bit, lower_part, upper_part)
        kept = jnp.where(upper_bit, upper_part, lower_part)
        arrived, arrived_totals = from_partner((outgoing, totals), "narrow", level)
        mixture = kept + arrived
        totals = totals + arrived_totals
    divisor = jnp.repeat(
        jnp.transpose(totals, (0, 2, 1)).reshape(row_count, local_heads),
        mixture.shape[1] // local_heads,
        axis=1,
    )
    attended = (mixture / divisor).astype(jnp.bfloat16)
    projected = jnp.dot(
        lax.all_gather(attended, "narrow", axis=1, tiled=True),
        out_weight,
        preferred_element_type=jnp.float32,
    )
    residual = (
        layer_rows.reshape(row_count, feature_share).astype(jnp.float32) + projected
    ).astype(jnp.bfloat16)
    outgoing_rows = route_rows(residual, counts, canvases, slot_cap, groups, BAL)
    incoming = lax.all_to_all(outgoing_rows, "wide", split_axis=0, concat_axis=0, tiled=True)
    balanced = jnp.sum(incoming.astype(jnp.float32), axis=0).astype(jnp.bfloat16)
    return feed_forward(balanced, ffn_gain, w_gate, w_up, w_down)


def solution(mesh):
    return jax.shard_map(
        per_device,
        mesh=mesh,
        in_specs=(
            P(("rep", "wide"), None, "narrow"),
            P(("rep", "wide"), None, "narrow"),
            P(("rep", "wide"), None),
            P("rep"),
            P(("rep", "wide"), "narrow", None),
            P(("rep", "wide"), "narrow", None),
            P(None, "narrow"),
            P(),
            P("narrow", None),
            P("narrow", None),
            P("narrow", None),
        ),
        out_specs=P(("rep", "wide"), "narrow"),
        check_vma=False,
    )
```

profile of v0, /device:TPU:0, one launch (start us, length us, event | category | flops | bytes accessed | tf_op | source)
XLA Modules:
  0.0 227.7 jit_solution(1920225434575340196)
XLA Ops:
  6.5 0.0 all-gather.4.cloned.1.call-start
  6.5 0.7 convert_element_type.46
  7.2 1.1 reshape.231
  8.3 0.3 fusion.32
  8.7 0.5 multiply_cosine_fusion
  9.2 0.1 subtract_convert_fusion
  9.3 5.0 %multiply_reduce_fusion = (f32[2,4,120]{2,1,0:T(4,128)S(1)}, f32[2,4,120,2048]{3,2,1,0:T(8,128)S(1)}) fusion(bf16[2,4,2048,128]{3,2,1,0:T(8,128)(2,1)} %bitcast.28, bf16[2,120,4,64]{3,1,2,0:T(8,128)(2,1)S(1)} %get-tuple-element.8, bf16[2,120,4,64]{3,1,2,0:T(8,128)(2,1)S(1)} %get-tuple-element.7), kind=kOutput, calls=%fused_computation.2 | convolution fusion | flops 507739200 | bytes 12308224 | tf_op jit(solution)/shard_map/crhd,chpd->chrp/dot_general | solution.py:117
  14.3 0.0 copy-start
  14.4 1.4 fusion
  15.8 0.8 copy-done
  16.5 0.0 copy-start.5
  16.5 0.0 copy-start.4
  16.5 1.8 fusion.10
  18.4 0.1 copy.25
  18.5 0.1 copy.28
  18.6 0.3 broadcast_in_dim.55
  18.9 0.8 fusion.15
  19.7 0.0 all-gather.4.cloned.1.call-update
  19.7 0.0 all-gather.6.cloned.1.call-start
  19.8 0.0 copy-done.5
  19.8 0.2 reduce-window.8
  20.0 0.1 convert_reduce_fusion
  20.1 0.1 min.38
  20.2 0.1 select_reduce_fusion
  20.3 0.1 reduce_sum.54
  20.4 51.6 %all-gather.4.cloned.1.call-done = bf16[240,4096]{1,0:T(8,128)(2,1)} async-done(((bf16[240,512]{1,0:T(8,128)(2,1)}), bf16[240,4096]{1,0:T(8,128)(2,1)}) %all-gather.4.cloned.1.call-update) | async-done | bytes 1966096 | tf_op jit(solution)/shard_map/all_gather | solution.py:149
  72.0 0.0 copy-done.4
  72.0 4.0 %fusion.13 = bf16[240,512]{1,0:T(8,128)(2,1)S(1)} fusion(bf16[240,4096]{1,0:T(8,128)(2,1)} %all-gather.4.cloned.1.call-done, bf16[4096,512]{1,0:T(8,128)(2,1)} %param.17, bf16[240,512]{1,0:T(8,128)(2,1)S(1)} %bitcast.35), kind=kOutput, calls=%fused_computation.17 | convolution fusion | flops 1007001600 | bytes 6651904 | tf_op jit(solution)/shard_map/dot_general | solution.py:148
  76.0 0.0 copy-start.3
  76.0 2.0 gather_fusion
  78.0 0.1 gather.7
  78.1 0.1 select_select_fusion
  78.3 4.0 %all_to_all.5 = bf16[2,150,512]{2,1,0:T(8,128)(2,1)S(1)} all-to-all(bf16[2,150,512]{2,1,0:T(8,128)(2,1)S(1)} %select_select_fusion), channel_id=1, replica_groups=mesh['rep'=2,'wide'=2,'narrow'=8] {'wide'}, dimensions={0} | all-to-all | bytes 614400 | tf_op jit(solution)/shard_map/all_to_all | solution.py:157
  82.3 0.7 reduce_sum.57
  83.0 0.0 all-gather.6.cloned.1.call-update
  83.0 0.2 all-gather.8.cloned.1.call-start
  83.2 0.0 copy-done.3
  83.3 39.7 %all-gather.6.cloned.1.call-done = bf16[150,4096]{1,0:T(8,128)(2,1)} async-done(((bf16[150,512]{1,0:T(8,128)(2,1)}), bf16[150,4096]{1,0:T(8,128)(2,1)}) %all-gather.6.cloned.1.call-update) | async-done | bytes 1228816 | tf_op jit(solution)/shard_map/all_gather | solution.py:61
  123.0 1.6 fusion.6
  124.6 0.0 copy-start.2
  124.6 9.4 %fusion.17 = f32[150,1536]{1,0:T(8,128)S(1)} fusion(bf16[1536,4096]{1,0:T(8,128)(2,1)} %param.19, bf16[150,4096]{1,0:T(8,128)(2,1)} %all-gather.6.cloned.1.call-done, f32[4096]{0:T(1024)S(1)} %convert_element_type.52, f32[150]{0:T(256)S(1)} %add_rsqrt_fusion), kind=kOutput, calls=%fused_computation.24 | convolution fusion | flops 1889894400 | bytes 14750296 | tf_op jit(solution)/shard_map/dot_general | solution.py:68
  134.0 0.0 copy-done.2
  134.0 0.0 copy-start.1
  134.0 9.8 %fusion.9 = bf16[150,1536]{1,0:T(8,128)(2,1)} fusion(bf16[1536,4096]{1,0:T(8,128)(2,1)} %param.20, f32[150,1536]{1,0:T(8,128)S(1)} %fusion.17, bf16[150,4096]{1,0:T(8,128)(2,1)S(1)} %copy-done.2, f32[4096]{0:T(1024)S(1)} %convert_element_type.52, f32[150]{0:T(256)S(1)} %add_rsqrt_fusion), kind=kOutput, calls=%fused_computation.14 | convolution fusion | flops 1891276800 | bytes 15211096 | tf_op jit(solution)/shard_map/dot_general | solution.py:69
  143.9 0.0 all-gather.8.cloned.1.call-update
  143.9 66.6 %all-gather.8.cloned.1.call-done = bf16[150,12288]{1,0:T(8,128)(2,1)} async-done(((bf16[150,1536]{1,0:T(8,128)(2,1)}), bf16[150,12288]{1,0:T(8,128)(2,1)}) %all-gather.8.cloned.1.call-update) | async-done | bytes 3686416 | tf_op jit(solution)/shard_map/all_gather | solution.py:72
  210.4 0.0 copy-done.1
  210.5 10.7 %fusion.14 = bf16[150,512]{1,0:T(8,128)(2,1)} fusion(bf16[150,12288]{1,0:T(8,128)(2,1)} %all-gather.8.cloned.1.call-done, bf16[512,12288]{1,0:T(8,128)(2,1)} %param.21, bf16[150,512]{1,0:T(8,128)(2,1)S(1)} %copy-done.1), kind=kOutput, calls=%fused_computation.19 | convolution fusion | flops 1887667200 | bytes 16576512 | tf_op jit(solution)/shard_map/dot_general | solution.py:71
  (8 shorter events, 0.1 us)
Async XLA Ops:
  6.5 65.5 %all-gather.4.cloned.1.call-start = ((), (), s32[]{:S(2)}) async-start(), calls=%async_computation.1 | async-start | bytes 2211840 | tf_op jit(solution)/shard_map/all_gather | solution.py:149
  14.3 2.2 copy-start
  16.5 3.3 %copy-start.5 = (s32[4]{0:T(128)S(1)}, s32[4]{0:T(128)}, u32[]{:S(2)}) copy-start(s32[4]{0:T(128)} %param.14) | copy-start | bytes 52
  16.5 55.5 %copy-start.4 = (bf16[2,120,512]{2,1,0:T(8,128)(2,1)S(1)}, bf16[2,120,512]{2,1,0:T(8,128)(2,1)}, u32[]{:S(2)}) copy-start(bf16[2,120,512]{2,1,0:T(8,128)(2,1)} %param.12) | copy-start | bytes 737284
  19.7 103.2 %all-gather.6.cloned.1.call-start = ((), (), s32[]{:S(2)}) async-start(), calls=%async_computation.2 | async-start | bytes 1400832 | tf_op jit(solution)/shard_map/all_gather | solution.py:61
  76.0 7.2 %copy-start.3 = (bf16[4096]{0:T(1024)(128)(2,1)S(1)}, bf16[4096]{0:T(1024)(128)(2,1)}, u32[]{:S(2)}) copy-start(bf16[4096]{0:T(1024)(128)(2,1)} %param.18) | copy-start | bytes 24580
  83.0 127.4 %all-gather.8.cloned.1.call-start = ((), (), s32[]{:S(2)}) async-start(), calls=%async_computation.3 | async-start | bytes 4202496 | tf_op jit(solution)/shard_map/all_gather | solution.py:72
  124.6 9.4 %copy-start.2 = (bf16[150,4096]{1,0:T(8,128)(2,1)S(1)}, bf16[150,4096]{1,0:T(8,128)(2,1)}, u32[]{:S(2)}) copy-start(bf16[150,4096]{1,0:T(8,128)(2,1)} %all-gather.6.cloned.1.call-done) | copy-start | bytes 3686404
  134.0 76.4 %copy-start.1 = (bf16[150,512]{1,0:T(8,128)(2,1)S(1)}, bf16[150,512]{1,0:T(8,128)(2,1)}, u32[]{:S(2)}) copy-start(bf16[150,512]{1,0:T(8,128)(2,1)} %reduce_sum.57) | copy-start | bytes 460804
Sparse Core Ops, SparseCore 0:
  19.9 52.1 all-gather.3
  83.1 39.7 all-gather.5
  144.0 66.3 all-gather.7
where the time goes:
time: 228 us
  waiting for transfers between devices  158 us (69%)
  matrix products  40.8 us (18%)
  between operations  13.3 us (6%)
  other arithmetic  6.48 us (3%)
  local copies, waits for them, and re-layouts  5.03 us (2%)
  blocking collectives  3.97 us (2%)
    all_gather x1, waiting for transfers between devices, feed_forward(): lax.all_gather(activated, 'narrow', axis=1, tiled=True)  66.6 us
    all_gather x1, waiting for transfers between devices, per_device(): lax.all_gather(attended, 'narrow', axis=1, tiled=True)  51.6 us
    all_gather x1, waiting for transfers between devices, feed_forward(): lax.all_gather(residual, 'narrow', axis=1, tiled=True).astype(jnp.float32)  39.7 us
    dot_general x1, matrix products, feed_forward(): lax.dot_general(lax.all_gather(activated, 'narrow', axis=1, tiled=True),...  10.7 us
    dot_general x1, matrix products, feed_forward(): lax.dot_general(normed, w_up, contract, preferred_element_type=jnp.float32)  9.85 us
    dot_general x1, matrix products, feed_forward(): lax.dot_general(normed, w_gate, contract, preferred_element_type=jnp.floa...  9.4 us
    dot_general x1, matrix products, per_device(): jnp.einsum('crhd,chpd->chrp', rotated, key_blocks, preferred_element_type...  5.03 us
  transfers between devices with their start and end apart: 3, of which 3 were waited for; matrix products, arithmetic and copies ran while one was open for 0% of the time, Pallas kernels for 0%

commit v1 on v0

--- a/solution.py
+++ b/solution.py
@@ -1,11 +1,16 @@
+import functools
+
 import jax
 import jax.numpy as jnp
 from jax import lax
+from jax.experimental import pallas as pl
+from jax.experimental.pallas import tpu as pltpu
 from jax.sharding import PartitionSpec as P
 
 D = 4096
 HEAD = 128
 BAL = 150
+MESH = pl.DeviceIdType.MESH
 
 
 epsilon = 1e-05
@@ -32,9 +37,16 @@
     )
 
 
+def prefix_sum(counts):
+    index = jnp.arange(counts.shape[0], dtype=jnp.int32)
+    return jnp.sum(
+        jnp.where(index[None, :] <= index[:, None], counts[None, :], 0), axis=1, dtype=jnp.int32
+    )
+
+
 def balanced_slots(counts, canvases, slot_cap, groups, share):
     canvas_total = counts.shape[0]
-    canvas_end = jnp.cumsum(counts, dtype=jnp.int32)
+    canvas_end = prefix_sum(counts)
     canvas_start = canvas_end - counts
     global_slot = jnp.arange(groups * share, dtype=jnp.int32)
     canvas_of = jnp.sum(
@@ -75,6 +87,269 @@
         preferred_element_type=jnp.float32,
     )
     return (residual.astype(jnp.float32) + output).astype(jnp.bfloat16)
+
+
+def dot(a, b):
+    return jnp.dot(a, b, preferred_element_type=jnp.float32)
+
+
+def dot_t(a, b):
+    return lax.dot_general(a, b, (((1,), (1,)), ((), ())), preferred_element_type=jnp.float32)
+
+
+def rest_kernel(
+    levels,
+    chunks,
+    att_ref,
+    rows_ref,
+    pick_ref,
+    gain_ref,
+    wo_hbm,
+    wg_hbm,
+    wu_hbm,
+    wd_hbm,
+    out_ref,
+    wo,
+    wg,
+    wu,
+    wd,
+    other_att,
+    other_rows,
+    att_all,
+    bal_all,
+    act_all,
+    gate_acc,
+    up_acc,
+    out_acc,
+    w_sem,
+    swap_send,
+    swap_recv,
+    a_send,
+    a_recv,
+    b_send,
+    b_recv,
+    c_send,
+    c_recv,
+):
+    me = lax.axis_index("narrow")
+    wide = lax.axis_index("wide")
+    z, x = me // 2, me % 2
+    far = z // (levels // 2)
+    mirrored = z * (1 - far) + (levels - 1 - z) * far
+    width = att_ref.shape[1]
+    hidden = wg.shape[0]
+    chunk = hidden // chunks
+
+    loads = [
+        pltpu.make_async_copy(src, dst, w_sem.at[i])
+        for i, (src, dst) in enumerate(((wo_hbm, wo), (wg_hbm, wg), (wu_hbm, wu), (wd_hbm, wd)))
+    ]
+    for load in loads:
+        load.start()
+
+    barrier = pltpu.get_barrier_semaphore()
+
+    def greet(axis, index):
+        pl.semaphore_signal(barrier, inc=1, device_id={axis: index}, device_id_type=MESH)
+
+    greet("wide", 1 - wide)
+    greet("narrow", 2 * z + 1 - x)
+    pl.when(z < levels - 1)(lambda: greet("narrow", me + 2))
+    pl.when(z > 0)(lambda: greet("narrow", me - 2))
+    pl.semaphore_wait(barrier, 3 + (z + levels - 2) // (levels - 1) - z // (levels - 1))
+
+    swaps = [
+        pltpu.make_async_remote_copy(
+            src_ref=src,
+            dst_ref=dst,
+            send_sem=swap_send.at[i],
+            recv_sem=swap_recv.at[i],
+            device_id={"wide": 1 - wide},
+            device_id_type=MESH,
+        )
+        for i, (src, dst) in enumerate(((att_ref, other_att), (rows_ref, other_rows)))
+    ]
+    for swap in swaps:
+        swap.start()
+
+    def column(k):
+        if k == 0:
+            return z
+        near = 1 - mirrored if k == 1 else k
+        return near * (1 - far) + (levels - 1 - near) * far
+
+    sent = []
+
+    def spread(ref, send, recv, k, c):
+        level = column(k)
+        slot = 2 * level + x
+
+        def copy(way, target):
+            return pltpu.make_async_remote_copy(
+                src_ref=ref.at[slot, c],
+                dst_ref=ref.at[slot, c],
+                send_sem=send.at[k, c, way],
+                recv_sem=recv.at[slot, c],
+                device_id={"narrow": target},
+                device_id_type=MESH,
+            )
+
+        across, up, down = copy(0, 2 * z + 1 - x), copy(1, me + 2), copy(2, me - 2)
+        go_up = jnp.logical_and(level <= z, z < levels - 1)
+        go_down = jnp.logical_and(level >= z, z > 0)
+        pl.when(go_up)(up.start)
+        pl.when(go_down)(down.start)
+        across.start()
+        sent.extend(((go_up, up), (go_down, down), (None, across)))
+
+    def arrive(ref, recv, slot, c):
+        pltpu.make_async_copy(ref.at[slot, c], ref.at[slot, c], recv.at[slot, c]).wait()
+
+    def gather(ref, send, recv, pieces, use, own_sent=False):
+        if not own_sent:
+            for c in range(pieces):
+                spread(ref, send, recv, 0, c)
+        for c in range(pieces):
+            use(me, c, c == 0)
+        order = [(1, 0), (0, 1)]
+        for k in range(2, levels):
+            order += [(k, 0), (k - 1, 1)]
+        order += [(levels - 1, 1)]
+        for k, other in order:
+            slot = 2 * column(k) + (1 - x if other else x)
+            for c in range(pieces):
+                arrive(ref, recv, slot, c)
+                if not other:
+                    spread(ref, send, recv, k, c)
+                use(slot, c, False)
+
+    def picked(mine, theirs):
+        return dot(pick_ref[wide], mine[...]) + dot(pick_ref[1 - wide], theirs[...])
+
+    swaps[0].wait()
+    att_all[me, 0] = picked(att_ref, other_att).astype(jnp.bfloat16)
+
+    def project(slot, c, first):
+        part = dot(att_all[slot, c], wo[pl.ds(pl.multiple_of(slot * width, width), width), :])
+        if first:
+            swaps[1].wait()
+            out_acc[...] = picked(rows_ref, other_rows) + part
+        else:
+            out_acc[...] += part
+
+    spread(att_all, a_send, a_recv, 0, 0)
+    loads[0].wait()
+    gather(att_all, a_send, a_recv, 1, project, own_sent=True)
+
+    balanced = out_acc[...].astype(jnp.bfloat16)
+    bal_all[me, 0] = balanced
+    spread(bal_all, b_send, b_recv, 0, 0)
+    loads[1].wait()
+    loads[2].wait()
+    squares = []
+
+    def expand(slot, c, first):
+        block = bal_all[slot, c].astype(jnp.float32)
+        squares.append(jnp.sum(block * block, axis=1, keepdims=True))
+        columns = pl.ds(pl.multiple_of(slot * width, width), width)
+        scaled = (block * gain_ref[:, columns].astype(jnp.float32)).astype(jnp.bfloat16)
+        for j in range(chunks):
+            part = pl.ds(j * chunk, chunk)
+            gate = dot_t(scaled, wg[part, columns])
+            up = dot_t(scaled, wu[part, columns])
+            if first:
+                gate_acc[:, part] = gate
+                up_acc[:, part] = up
+            else:
+                gate_acc[:, part] += gate
+                up_acc[:, part] += up
+
+    gather(bal_all, b_send, b_recv, 1, expand, own_sent=True)
+
+    scale = lax.rsqrt(sum(squares) / (width * 2 * levels) + epsilon)
+    for c in range(chunks):
+        part = pl.ds(c * chunk, chunk)
+        gate = gate_acc[:, part] * scale
+        up = up_acc[:, part] * scale
+        act_all[me, c] = (gate / (1.0 + jnp.exp(-gate)) * up).astype(jnp.bfloat16)
+        spread(act_all, c_send, c_recv, 0, c)
+
+    out_acc[...] = bal_all[me, 0].astype(jnp.float32)
+    loads[3].wait()
+
+    def contract(slot, c, first):
+        columns = pl.ds(pl.multiple_of(slot * hidden + c * chunk, chunk), chunk)
+        out_acc[...] += dot_t(act_all[slot, c], wd[:, columns])
+
+    gather(act_all, c_send, c_recv, chunks, contract, own_sent=True)
+    out_ref[...] = out_acc[: out_ref.shape[0], :].astype(jnp.bfloat16)
+    for condition, copy in sent:
+        if condition is None:
+            copy.wait_send()
+        else:
+            pl.when(condition)(copy.wait_send)
+
+
+def rest(attended, layer_rows, counts, ffn_gain, out_weight, w_gate, w_up, w_down, slot_cap):
+    groups, narrow_count = lax.axis_size("wide"), lax.axis_size("narrow")
+    row_count, width = attended.shape
+    hidden = w_gate.shape[0]
+    levels = narrow_count // 2
+    chunks = 3
+    padded = -(-BAL // 16) * 16
+    canvas_end = prefix_sum(counts)
+    canvas_start = canvas_end - counts
+    slots = jnp.arange(row_count * groups, dtype=jnp.int32)
+    canvas = slots // slot_cap
+    chosen = canvas[:, None] == jnp.arange(counts.shape[0], dtype=jnp.int32)[None, :]
+    within = slots % slot_cap
+    start = jnp.sum(jnp.where(chosen, canvas_start[None, :], 0), axis=1, dtype=jnp.int32)
+    count = jnp.sum(jnp.where(chosen, counts[None, :], 0), axis=1, dtype=jnp.int32)
+    place = jnp.where(within < count, start + within - lax.axis_index("wide") * BAL, -1)
+    place = place.reshape(groups, 1, row_count)
+    target = jnp.arange(padded, dtype=jnp.int32)[None, :, None]
+    pick = jnp.logical_and(place == target, target < BAL).astype(jnp.bfloat16)
+
+    vmem = pl.BlockSpec(memory_space=pltpu.VMEM)
+    hbm = pl.BlockSpec(memory_space=pl.ANY)
+    chunk = hidden // chunks
+    sems = pltpu.SemaphoreType.DMA
+    return pl.pallas_call(
+        functools.partial(rest_kernel, levels, chunks),
+        out_shape=jax.ShapeDtypeStruct((BAL, width), jnp.bfloat16),
+        in_specs=[vmem] * 4 + [hbm] * 4,
+        out_specs=vmem,
+        scratch_shapes=[
+            pltpu.VMEM(out_weight.shape, jnp.bfloat16),
+            pltpu.VMEM(w_gate.shape, jnp.bfloat16),
+            pltpu.VMEM(w_up.shape, jnp.bfloat16),
+            pltpu.VMEM(w_down.shape, jnp.bfloat16),
+            pltpu.VMEM((row_count, width), jnp.bfloat16),
+            pltpu.VMEM((row_count, width), jnp.bfloat16),
+            pltpu.VMEM((narrow_count, 1, padded, width), jnp.bfloat16),
+            pltpu.VMEM((narrow_count, 1, padded, width), jnp.bfloat16),
+            pltpu.VMEM((narrow_count, chunks, padded, chunk), jnp.bfloat16),
+            pltpu.VMEM((padded, hidden), jnp.float32),
+            pltpu.VMEM((padded, hidden), jnp.float32),
+            pltpu.VMEM((padded, width), jnp.float32),
+            sems((4,)),
+            sems((2,)),
+            sems((2,)),
+            sems((levels, 1, 3)),
+            sems((narrow_count, 1)),
+            sems((levels, 1, 3)),
+            sems((narrow_count, 1)),
+            sems((levels, chunks, 3)),
+            sems((narrow_count, chunks)),
+        ],
+        compiler_params=pltpu.CompilerParams(
+            collective_id=0, has_side_effects=True, vmem_limit_bytes=60 * 2**20
+        ),
+    )(attended, layer_rows, pick, ffn_gain.reshape(1, -1), out_weight, w_gate, w_up, w_down)
+
+
+def fits_kernel(narrow_count, groups, width, hidden):
+    return narrow_count == 8 and groups == 2 and width % 128 == 0 and hidden % 384 == 0
 
 
 def per_device(
@@ -145,6 +420,18 @@
         axis=1,
     )
     attended = (mixture / divisor).astype(jnp.bfloat16)
+    if fits_kernel(narrow_count, groups, feature_share, w_gate.shape[0]):
+        return rest(
+            attended,
+            layer_rows.reshape(row_count, feature_share),
+            counts,
+            ffn_gain,
+            out_weight,
+            w_gate,
+            w_up,
+            w_down,
+            slot_cap,
+        )
     projected = jnp.dot(
         lax.all_gather(attended, "narrow", axis=1, tiled=True),
         out_weight,

time: 228 us -> 109 us (0.48)
  waiting for transfers between devices: 158 us -> 0 us
  Pallas kernels: 0 us -> 90.2 us
  matrix products: 40.8 us -> 6.89 us
  between operations: 13.3 us -> 0.08 us
  blocking collectives: 3.97 us -> 0 us
    all_gather x3 -> x0, waiting for transfers between devices: 158 us -> none  [the longest x1 66.6 us: feed_forward(): lax.all_gather(activated, 'narrow', axis=1, tiled=True)]
    pallas_call x0 -> x1, Pallas kernels: none -> 90.2 us  [rest(): pl.pallas_call(functools.partial(rest_kernel, levels, chunks), out_shape=...]
    dot_general x4 -> x0, matrix products: 33.9 us -> none  [the longest x1 10.7 us: feed_forward(): lax.dot_general(lax.all_gather(activated, 'narrow', axis=1, tiled=True),...]
    all_to_all x1 -> x0, blocking collectives: 3.97 us -> none  [per_device(): lax.all_to_all(outgoing_rows, 'wide', split_axis=0, concat_axis=0, tiled=...]
  transfers between devices with their start and end apart: 3 -> 0, of which waited for: 3 -> 0; matrix products, arithmetic and copies ran while one was open for 0% -> 0% of each run, Pallas kernels for 0% -> 0%
where the time goes in v1:
time: 109 us
  Pallas kernels  90.2 us (83%)
  matrix products  6.89 us (6%)
  other arithmetic  6.49 us (6%)
  local copies, waits for them, and re-layouts  5.07 us (5%)
    pallas_call x1, Pallas kernels, rest(): pl.pallas_call(functools.partial(rest_kernel, levels, chunks), out_shape=...  90.2 us
    dot_general x1, matrix products, per_device(): jnp.einsum('crhd,chpd->chrp', rotated, key_blocks, preferred_element_type...  5.18 us

profile of v1, /device:TPU:0, one launch (start us, length us, event | category | flops | bytes accessed | tf_op | source)
XLA Modules:
  0.0 108.7 jit_solution(11857331831356546301)
XLA Ops:
  0.0 0.8 select_reduce_fusion.2
  0.8 0.7 sub.36
  1.5 0.7 convert_element_type.14
  2.1 0.7 select_reduce_fusion
  2.9 0.1 reduce_sum.45
  3.0 0.1 reduce_sum.42
  3.1 1.3 %reshape.91.gain_ref = bf16[1,4096]{1,0:T(2,128)(2,1)} reshape(bf16[4096]{0:T(1024)(128)(2,1)} %param.18) | data formatting | bytes 16384 | tf_op jit(solution)/shard_map/reshape | solution.py:348
  4.4 0.8 fusion.11.pick_ref
  5.2 0.5 multiply_cosine_fusion
  5.7 1.1 %reshape.93 = f32[2,120,4,128]{3,2,1,0:T(4,128)S(1)} reshape(bf16[2,120,512]{2,1,0:T(8,128)(2,1)} %param.11) | data formatting | bytes 737280 | tf_op jit(solution)/shard_map/reshape | solution.py:387
  6.8 0.3 fusion.21
  7.1 0.1 subtract_convert_fusion
  7.2 0.0 copy-start
  7.2 5.2 %multiply_reduce_fusion = (f32[2,4,120]{2,1,0:T(4,128)S(1)}, f32[2,4,120,2048]{3,2,1,0:T(8,128)S(1)}) fusion(bf16[2,4,2048,128]{3,2,1,0:T(8,128)(2,1)} %bitcast.18, bf16[2,120,4,64]{3,1,2,0:T(8,128)(2,1)S(1)} %get-tuple-element.8, bf16[2,120,4,64]{3,1,2,0:T(8,128)(2,1)S(1)} %get-tuple-element.7), kind=kOutput, calls=%fused_computation.1 | convolution fusion | flops 507739200 | bytes 12308224 | tf_op jit(solution)/shard_map/crhd,chpd->chrp/dot_general | solution.py:392
  12.4 1.4 %fusion = f32[2,4,120]{2,1,0:T(4,128)S(1)} fusion(f32[2,4,120,2048]{3,2,1,0:T(8,128)S(1)} %get-tuple-element.14, f32[2,4,120]{2,1,0:T(4,128)S(1)} %get-tuple-element.13), kind=kLoop, calls=%fused_computation.2 | loop fusion | flops 5897280 | bytes 7872000 | tf_op jit(solution)/shard_map/reduce_sum | solution.py:400
  13.8 0.0 copy-done
  13.9 1.7 %fusion.6 = f32[2,120,4,128]{3,1,2,0:T(8,128)S(1)} fusion(bf16[2,4,2048,128]{3,2,1,0:T(8,128)(2,1)S(1)} %bitcast.19, f32[2,4,120,2048]{3,2,1,0:T(8,128)S(1)} %get-tuple-element.14, f32[2,4,120]{2,1,0:T(4,128)S(1)} %get-tuple-element.13), kind=kOutput, calls=%fused_computation.7 | convolution fusion | flops 509214720 | bytes 12553984 | tf_op jit(solution)/shard_map/chrp,chpd->crhd/dot_general | solution.py:401
  15.6 0.1 copy.26
  15.7 0.1 copy.29
  15.8 0.3 broadcast_in_dim.50
  16.2 0.8 fusion.9.att_ref
  16.9 90.2 %shard_map.109 = bf16[150,512]{1,0:T(8,128)(2,1)} custom-call(bf16[240,512]{1,0:T(8,128)(2,1)} %fusion.9.att_ref, bf16[240,512]{1,0:T(8,128)(2,1)} %bitcast.23, bf16[2,160,240]{2,1,0:T(8,128)(2,1)} %fusion.11.pick_ref, bf16[1,4096]{1,0:T(2,128)(2,1)} %reshape.91.gain_ref, bf16[4096,512]{1,0:T(8,128)(2,1)} %wo_hbm.1, bf16[1536,4096]{1,0:T(8,128)(2,1)} %wg_hbm.1, ...), custom_call_target="tpu_custom_call" | custom-call | tf_op jit(solution)/shard_map/pallas_call | solution.py:317
  107.1 1.6 %copy.42 = bf16[150,512]{1,0:T(8,128)(2,1)} copy(bf16[150,512]{1,0:T(8,128)(2,1)} %shard_map.109) | data formatting | bytes 307200
  (4 shorter events, 0.0 us)
Async XLA Ops:
  7.2 6.6 %copy-start = (bf16[2,8192,128]{2,1,0:T(8,128)(2,1)S(1)}, bf16[2,8192,128]{2,1,0:T(8,128)(2,1)}, u32[]{:S(2)}) copy-start(bf16[2,8192,128]{2,1,0:T(8,128)(2,1)} %param.16) | copy-start | bytes 12582916

commit v2 on v1

--- a/solution.py
+++ b/solution.py
@@ -100,9 +100,10 @@
 def rest_kernel(
     levels,
     chunks,
+    slot_cap,
+    counts_ref,
     att_ref,
     rows_ref,
-    pick_ref,
     gain_ref,
     wo_hbm,
     wg_hbm,
@@ -144,8 +145,7 @@
         pltpu.make_async_copy(src, dst, w_sem.at[i])
         for i, (src, dst) in enumerate(((wo_hbm, wo), (wg_hbm, wg), (wu_hbm, wu), (wd_hbm, wd)))
     ]
-    for load in loads:
-        load.start()
+    loads[0].start()
 
     barrier = pltpu.get_barrier_semaphore()
 
@@ -180,35 +180,41 @@
 
     sent = []
 
-    def spread(ref, send, recv, k, c):
+    def spread(ref, send, recv, k, c, other, shared):
         level = column(k)
-        slot = 2 * level + x
+        slot = 2 * level + (1 - x if other else x)
 
         def copy(way, target):
             return pltpu.make_async_remote_copy(
                 src_ref=ref.at[slot, c],
                 dst_ref=ref.at[slot, c],
-                send_sem=send.at[k, c, way],
+                send_sem=send.at[k, c, 3 * other + way],
                 recv_sem=recv.at[slot, c],
                 device_id={"narrow": target},
                 device_id_type=MESH,
             )
 
-        across, up, down = copy(0, 2 * z + 1 - x), copy(1, me + 2), copy(2, me - 2)
-        go_up = jnp.logical_and(level <= z, z < levels - 1)
-        go_down = jnp.logical_and(level >= z, z > 0)
-        pl.when(go_up)(up.start)
-        pl.when(go_down)(down.start)
-        across.start()
-        sent.extend(((go_up, up), (go_down, down), (None, across)))
+        low, high = level == 0, level == levels - 1
+        go_up, go_down = z < levels - 1, z > 0
+        if other:
+            go_up, go_down = go_up & low, go_down & high
+        else:
+            go_up, go_down = go_up & (level <= z), go_down & (level >= z)
+        moves = [(go_up, copy(0, me + 2)), (go_down, copy(1, me - 2))]
+        if not other:
+            across = (level == z) | ((level > 0) & (level < levels - 1)) if shared else None
+            moves.append((across, copy(2, 2 * z + 1 - x)))
+        for condition, move in moves:
+            if condition is None:
+                move.start()
+            else:
+                pl.when(condition)(move.start)
+        sent.extend(moves)
 
     def arrive(ref, recv, slot, c):
         pltpu.make_async_copy(ref.at[slot, c], ref.at[slot, c], recv.at[slot, c]).wait()
 
-    def gather(ref, send, recv, pieces, use, own_sent=False):
-        if not own_sent:
-            for c in range(pieces):
-                spread(ref, send, recv, 0, c)
+    def gather(ref, send, recv, pieces, use):
         for c in range(pieces):
             use(me, c, c == 0)
         order = [(1, 0), (0, 1)]
@@ -218,43 +224,76 @@
         for k, other in order:
             slot = 2 * column(k) + (1 - x if other else x)
             for c in range(pieces):
+                shared = c >= pieces // 2
                 arrive(ref, recv, slot, c)
-                if not other:
-                    spread(ref, send, recv, k, c)
+                if shared or not other:
+                    spread(ref, send, recv, k, c, other, shared)
                 use(slot, c, False)
 
+    starts = [jnp.int32(0)]
+    for i in range(counts_ref.shape[0] - 1):
+        starts.append(starts[i] + counts_ref[i])
+    canvases = att_ref.shape[0] // slot_cap
+    shape = (out_acc.shape[0], att_ref.shape[0])
+    row = lax.broadcasted_iota(jnp.int32, shape, 0) + wide * out_ref.shape[0]
+    slot_index = lax.broadcasted_iota(jnp.int32, shape, 1)
+    inside = lax.broadcasted_iota(jnp.int32, shape, 0) < out_ref.shape[0]
+
+    def pick(group):
+        found = jnp.zeros(shape, jnp.float32)
+        for i in range(canvases):
+            start = starts[i] * (1 - group) + starts[canvases + i] * group
+            count = counts_ref[i] * (1 - group) + counts_ref[canvases + i] * group
+            within = slot_index - i * slot_cap
+            live = (within >= 0) & (within < slot_cap) & (within < count) & inside
+            found += jnp.where(live & (start + within == row), 1.0, 0.0)
+        return found.astype(jnp.bfloat16)
+
+    pick_mine, pick_theirs = pick(wide), pick(1 - wide)
+
     def picked(mine, theirs):
-        return dot(pick_ref[wide], mine[...]) + dot(pick_ref[1 - wide], theirs[...])
+        return dot(pick_mine, mine[...]) + dot(pick_theirs, theirs[...])
+
+    half = att_all.shape[3]
+    pieces = width // half
+
+    def put(ref, send, recv, value):
+        for c in range(pieces):
+            ref[me, c] = value[:, c * half : (c + 1) * half]
+            spread(ref, send, recv, 0, c, 0, c >= pieces // 2)
 
     swaps[0].wait()
-    att_all[me, 0] = picked(att_ref, other_att).astype(jnp.bfloat16)
+    put(att_all, a_send, a_recv, picked(att_ref, other_att).astype(jnp.bfloat16))
 
     def project(slot, c, first):
-        part = dot(att_all[slot, c], wo[pl.ds(pl.multiple_of(slot * width, width), width), :])
+        depth = pl.ds(pl.multiple_of(slot * width + c * half, half), half)
+        part = dot(att_all[slot, c], wo[depth, :])
         if first:
             swaps[1].wait()
             out_acc[...] = picked(rows_ref, other_rows) + part
         else:
             out_acc[...] += part
 
-    spread(att_all, a_send, a_recv, 0, 0)
     loads[0].wait()
-    gather(att_all, a_send, a_recv, 1, project, own_sent=True)
+    for load in loads[1:]:
+        load.start()
+    gather(att_all, a_send, a_recv, pieces, project)
 
     balanced = out_acc[...].astype(jnp.bfloat16)
-    bal_all[me, 0] = balanced
-    spread(bal_all, b_send, b_recv, 0, 0)
+    put(bal_all, b_send, b_recv, balanced)
+    out_acc[...] = balanced.astype(jnp.float32)
     loads[1].wait()
     loads[2].wait()
     squares = []
+    tile = 512 if hidden % 512 == 0 else 384
 
     def expand(slot, c, first):
         block = bal_all[slot, c].astype(jnp.float32)
         squares.append(jnp.sum(block * block, axis=1, keepdims=True))
-        columns = pl.ds(pl.multiple_of(slot * width, width), width)
-        scaled = (block * gain_ref[:, columns].astype(jnp.float32)).astype(jnp.bfloat16)
-        for j in range(chunks):
-            part = pl.ds(j * chunk, chunk)
+        columns = pl.ds(pl.multiple_of(slot * width + c * half, half), half)
+        scaled = (block * gain_ref[:, columns]).astype(jnp.bfloat16)
+        for j in range(hidden // tile):
+            part = pl.ds(j * tile, tile)
             gate = dot_t(scaled, wg[part, columns])
             up = dot_t(scaled, wu[part, columns])
             if first:
@@ -264,7 +303,7 @@
                 gate_acc[:, part] += gate
                 up_acc[:, part] += up
 
-    gather(bal_all, b_send, b_recv, 1, expand, own_sent=True)
+    gather(bal_all, b_send, b_recv, pieces, expand)
 
     scale = lax.rsqrt(sum(squares) / (width * 2 * levels) + epsilon)
     for c in range(chunks):
@@ -272,16 +311,15 @@
         gate = gate_acc[:, part] * scale
         up = up_acc[:, part] * scale
         act_all[me, c] = (gate / (1.0 + jnp.exp(-gate)) * up).astype(jnp.bfloat16)
-        spread(act_all, c_send, c_recv, 0, c)
-
-    out_acc[...] = bal_all[me, 0].astype(jnp.float32)
+        spread(act_all, c_send, c_recv, 0, c, 0, c >= chunks // 2)
+
     loads[3].wait()
 
     def contract(slot, c, first):
         columns = pl.ds(pl.multiple_of(slot * hidden + c * chunk, chunk), chunk)
         out_acc[...] += dot_t(act_all[slot, c], wd[:, columns])
 
-    gather(act_all, c_send, c_recv, chunks, contract, own_sent=True)
+    gather(act_all, c_send, c_recv, chunks, contract)
     out_ref[...] = out_acc[: out_ref.shape[0], :].astype(jnp.bfloat16)
     for condition, copy in sent:
         if condition is None:
@@ -291,33 +329,21 @@
 
 
 def rest(attended, layer_rows, counts, ffn_gain, out_weight, w_gate, w_up, w_down, slot_cap):
-    groups, narrow_count = lax.axis_size("wide"), lax.axis_size("narrow")
+    narrow_count = lax.axis_size("narrow")
     row_count, width = attended.shape
     hidden = w_gate.shape[0]
     levels = narrow_count // 2
-    chunks = 3
+    chunks, pieces = hidden // 256, 2
     padded = -(-BAL // 16) * 16
-    canvas_end = prefix_sum(counts)
-    canvas_start = canvas_end - counts
-    slots = jnp.arange(row_count * groups, dtype=jnp.int32)
-    canvas = slots // slot_cap
-    chosen = canvas[:, None] == jnp.arange(counts.shape[0], dtype=jnp.int32)[None, :]
-    within = slots % slot_cap
-    start = jnp.sum(jnp.where(chosen, canvas_start[None, :], 0), axis=1, dtype=jnp.int32)
-    count = jnp.sum(jnp.where(chosen, counts[None, :], 0), axis=1, dtype=jnp.int32)
-    place = jnp.where(within < count, start + within - lax.axis_index("wide") * BAL, -1)
-    place = place.reshape(groups, 1, row_count)
-    target = jnp.arange(padded, dtype=jnp.int32)[None, :, None]
-    pick = jnp.logical_and(place == target, target < BAL).astype(jnp.bfloat16)
 
     vmem = pl.BlockSpec(memory_space=pltpu.VMEM)
     hbm = pl.BlockSpec(memory_space=pl.ANY)
     chunk = hidden // chunks
     sems = pltpu.SemaphoreType.DMA
     return pl.pallas_call(
-        functools.partial(rest_kernel, levels, chunks),
+        functools.partial(rest_kernel, levels, chunks, slot_cap),
         out_shape=jax.ShapeDtypeStruct((BAL, width), jnp.bfloat16),
-        in_specs=[vmem] * 4 + [hbm] * 4,
+        in_specs=[pl.BlockSpec(memory_space=pltpu.SMEM)] + [vmem] * 3 + [hbm] * 4,
         out_specs=vmem,
         scratch_shapes=[
             pltpu.VMEM(out_weight.shape, jnp.bfloat16),
@@ -326,8 +352,8 @@
             pltpu.VMEM(w_down.shape, jnp.bfloat16),
             pltpu.VMEM((row_count, width), jnp.bfloat16),
             pltpu.VMEM((row_count, width), jnp.bfloat16),
-            pltpu.VMEM((narrow_count, 1, padded, width), jnp.bfloat16),
-            pltpu.VMEM((narrow_count, 1, padded, width), jnp.bfloat16),
+            pltpu.VMEM((narrow_count, pieces, padded, width // pieces), jnp.bfloat16),
+            pltpu.VMEM((narrow_count, pieces, padded, width // pieces), jnp.bfloat16),
             pltpu.VMEM((narrow_count, chunks, padded, chunk), jnp.bfloat16),
             pltpu.VMEM((padded, hidden), jnp.float32),
             pltpu.VMEM((padded, hidden), jnp.float32),
@@ -335,21 +361,66 @@
             sems((4,)),
             sems((2,)),
             sems((2,)),
-            sems((levels, 1, 3)),
-            sems((narrow_count, 1)),
-            sems((levels, 1, 3)),
-            sems((narrow_count, 1)),
-            sems((levels, chunks, 3)),
+            sems((levels, pieces, 6)),
+            sems((narrow_count, pieces)),
+            sems((levels, pieces, 6)),
+            sems((narrow_count, pieces)),
+            sems((levels, chunks, 6)),
             sems((narrow_count, chunks)),
         ],
         compiler_params=pltpu.CompilerParams(
             collective_id=0, has_side_effects=True, vmem_limit_bytes=60 * 2**20
         ),
-    )(attended, layer_rows, pick, ffn_gain.reshape(1, -1), out_weight, w_gate, w_up, w_down)
+    )(
+        counts,
+        attended,
+        layer_rows,
+        ffn_gain.astype(jnp.float32).reshape(1, -1),
+        out_weight,
+        w_gate,
+        w_up,
+        w_down,
+    )
+
+
+def attend_kernel(heads, q_ref, cos_ref, sin_ref, k_ref, v_ref, o_ref):
+    length = k_ref.shape[1] // heads
+    for h in range(heads):
+        lanes = slice(h * HEAD, (h + 1) * HEAD)
+        spots = slice(h * length, (h + 1) * length)
+        query = q_ref[0, :, lanes].astype(jnp.float32)
+        turned = query * cos_ref[0] + pltpu.roll(query, HEAD // 2, 1) * sin_ref[0]
+        scores = dot_t(turned.astype(jnp.bfloat16), k_ref[0, spots, :]) * HEAD ** (-0.5)
+        exponent = jnp.exp(scores - jnp.max(scores, axis=1, keepdims=True))
+        total = jnp.sum(exponent, axis=1, keepdims=True)
+        mixture = dot(exponent.astype(jnp.bfloat16), v_ref[0, spots, :])
+        o_ref[0, :, lanes] = (mixture / total).astype(jnp.bfloat16)
+
+
+def attend(queries, positions, key_cache, value_cache):
+    canvases, slot_cap, width = queries.shape
+    heads = 2 if width % (2 * HEAD) == 0 else 1
+    steps = width // (heads * HEAD)
+    frequency = 500000.0 ** (-2.0 * jnp.arange(HEAD // 2, dtype=jnp.float32) / HEAD)
+    angles = positions.astype(jnp.float32)[..., None] * frequency
+    cosine, sine = jnp.cos(angles), jnp.sin(angles)
+    cosine = jnp.concatenate([cosine, cosine], axis=-1)
+    sine = jnp.concatenate([-sine, sine], axis=-1)
+    table = pl.BlockSpec((1, slot_cap, HEAD), lambda c, h: (c, 0, 0))
+    rows = pl.BlockSpec((1, slot_cap, heads * HEAD), lambda c, h: (c, 0, h))
+    cached = pl.BlockSpec((1, key_cache.shape[1] // steps, HEAD), lambda c, h: (c, h, 0))
+    return pl.pallas_call(
+        functools.partial(attend_kernel, heads),
+        grid=(canvases, steps),
+        in_specs=[rows, table, table, cached, cached],
+        out_specs=rows,
+        out_shape=jax.ShapeDtypeStruct(queries.shape, jnp.bfloat16),
+        compiler_params=pltpu.CompilerParams(vmem_limit_bytes=40 * 2**20),
+    )(queries, cosine, sine, key_cache, value_cache)
 
 
 def fits_kernel(narrow_count, groups, width, hidden):
-    return narrow_count == 8 and groups == 2 and width % 128 == 0 and hidden % 384 == 0
+    return narrow_count == 8 and groups == 2 and width % 256 == 0 and hidden % 768 == 0
 
 
 def per_device(
@@ -370,6 +441,18 @@
     narrow_count = lax.axis_size("narrow")
     groups = lax.axis_size("wide")
     row_count = canvases * slot_cap
+    if fits_kernel(narrow_count, groups, feature_share, w_gate.shape[0]):
+        return rest(
+            attend(queries, positions, key_cache, value_cache).reshape(row_count, feature_share),
+            layer_rows.reshape(row_count, feature_share),
+            counts,
+            ffn_gain,
+            out_weight,
+            w_gate,
+            w_up,
+            w_down,
+            slot_cap,
+        )
     group_size = max(1, narrow_count // head_count)
     local_heads = max(1, head_count // narrow_count)
     bit_steps = group_size.bit_length() - 1
@@ -420,18 +503,6 @@
         axis=1,
     )
     attended = (mixture / divisor).astype(jnp.bfloat16)
-    if fits_kernel(narrow_count, groups, feature_share, w_gate.shape[0]):
-        return rest(
-            attended,
-            layer_rows.reshape(row_count, feature_share),
-            counts,
-            ffn_gain,
-            out_weight,
-            w_gate,
-            w_up,
-            w_down,
-            slot_cap,
-        )
     projected = jnp.dot(
         lax.all_gather(attended, "narrow", axis=1, tiled=True),
         out_weight,

time: 109 us -> 97.7 us (0.90)
  matrix products: 6.89 us -> 0 us
  other arithmetic: 6.49 us -> 2.64 us
  Pallas kernels: 90.2 us -> 87.1 us
  local copies, waits for them, and re-layouts: 5.07 us -> 7.58 us
    dot_general x2 -> x0, matrix products: 6.89 us -> none  [the longest x1 5.18 us: per_device(): jnp.einsum('crhd,chpd->chrp', rotated, key_blocks, preferred_element_type...]
    unnamed x3 -> x9, local copies, waits for them, and re-layouts: 1.59 us -> 7.58 us
    pallas_call x1 -> x2, Pallas kernels: 90.2 us -> 87.1 us  [the longest x1 81.7 us: rest(): pl.pallas_call(functools.partial(rest_kernel, levels, chunks, slot_cap),...]
    reduce_sum x3 -> x0, other arithmetic: 2.94 us -> none  [the longest x1 1.43 us: per_device(): totals = jnp.sum(exponent, axis=3)]
    reshape x3 -> x0, local copies, waits for them, and re-layouts: 2.54 us -> none  [the longest x1 1.31 us: rest(): ffn_gain.reshape(1, -1)]
    convert_element_type x3 -> x1, other arithmetic: 2.21 us -> 0.68 us  [attend(): angles = positions.astype(jnp.float32)[..., None] * frequency]
    reshape x0 -> x1, other arithmetic: none -> 1.3 us  [rest(): ffn_gain.astype(jnp.float32).reshape(1, -1)]
where the time goes in v2:
time: 97.7 us; the launch traced here: 97.4 us
  Pallas kernels  87.1 us (89%)
  local copies, waits for them, and re-layouts  7.58 us (8%)
  other arithmetic  2.64 us (3%)
    pallas_call x1, Pallas kernels, rest(): pl.pallas_call(functools.partial(rest_kernel, levels, chunks, slot_cap),...  81.7 us
    unnamed x9, local copies, waits for them, and re-layouts  7.58 us
    pallas_call x1, Pallas kernels, attend(): pl.pallas_call(functools.partial(attend_kernel, heads), grid=(canvases, s...  5.35 us

profile of v2, /device:TPU:0, one launch (start us, length us, event | category | flops | bytes accessed | tf_op | source)
XLA Modules:
  0.0 97.4 jit_solution(3757526247318327348)
XLA Ops:
  0.0 0.7 convert_element_type.4
  0.7 0.5 fusion
  1.2 0.1 pad_maximum_fusion
  1.4 0.0 copy-start
  1.4 2.2 %copy-done = bf16[2,8192,128]{2,1,0:T(8,128)(2,1)S(1)} copy-done((bf16[2,8192,128]{2,1,0:T(8,128)(2,1)S(1)}, bf16[2,8192,128]{2,1,0:T(8,128)(2,1)}, u32[]{:S(2)}) %copy-start) | copy-done | bytes 4194328
  3.5 0.0 copy-start.1
  3.5 2.2 %copy-done.1 = bf16[2,8192,128]{2,1,0:T(8,128)(2,1)S(1)} copy-done((bf16[2,8192,128]{2,1,0:T(8,128)(2,1)S(1)}, bf16[2,8192,128]{2,1,0:T(8,128)(2,1)}, u32[]{:S(2)}) %copy-start.1) | copy-done | bytes 4194328
  5.7 0.0 copy-start.3
  5.7 0.9 copy-done.3
  6.7 5.4 %shard_map.109 = bf16[2,120,512]{2,1,0:T(8,128)(2,1)S(1)} custom-call(bf16[2,120,512]{2,1,0:T(8,128)(2,1)S(1)} %copy-done.3, f32[2,120,128]{2,1,0:T(8,128)S(1)} %get-tuple-element.8.cos_ref, f32[2,120,128]{2,1,0:T(8,128)S(1)} %get-tuple-element.9.sin_ref, bf16[2,8192,128]{2,1,0:T(8,128)(2,1)S(1)} %copy-done, bf16[2,8192,128]{2,1,0:T(8,128)(2,1)S(1)} %copy-done.1), custom_call_target="tpu_custom_call" | custom-call | tf_op jit(solution)/shard_map/pallas_call | solution.py:412
  12.0 0.0 copy-start.2
  12.0 0.7 copy-done.2
  12.7 1.3 %reshape.21 = f32[4096]{0:T(1024)} convert(bf16[4096]{0:T(1024)(128)(2,1)} %param.18) | non-fusion elementwise | flops 4096 | bytes 24576 | tf_op jit(solution)/shard_map/reshape | solution.py:378
  14.0 81.7 %shard_map.110 = bf16[150,512]{1,0:T(8,128)(2,1)} custom-call(s32[4]{0:T(128)} %counts_ref.1, bf16[240,512]{1,0:T(8,128)(2,1)} %bitcast.3, bf16[240,512]{1,0:T(8,128)(2,1)} %bitcast.4, f32[1,4096]{1,0:T(1,128)} %bitcast.5, bf16[4096,512]{1,0:T(8,128)(2,1)} %wo_hbm.1, bf16[1536,4096]{1,0:T(8,128)(2,1)} %wg_hbm.1, bf16[1536,4096]{1,0:T(8,128)(2,1)} %wu_hbm.1, ...), custom_call_target="tpu_custom_call" | custom-call | tf_op jit(solution)/shard_map/pallas_call | solution.py:343
  95.8 1.6 %copy.13 = bf16[150,512]{1,0:T(8,128)(2,1)} copy(bf16[150,512]{1,0:T(8,128)(2,1)} %shard_map.110) | data formatting | bytes 307200
  (1 shorter events, 0.0 us)
Async XLA Ops:
  1.4 2.2 %copy-start = (bf16[2,8192,128]{2,1,0:T(8,128)(2,1)S(1)}, bf16[2,8192,128]{2,1,0:T(8,128)(2,1)}, u32[]{:S(2)}) copy-start(bf16[2,8192,128]{2,1,0:T(8,128)(2,1)} %k_ref.1) | copy-start | bytes 12582916
  3.5 2.2 %copy-start.1 = (bf16[2,8192,128]{2,1,0:T(8,128)(2,1)S(1)}, bf16[2,8192,128]{2,1,0:T(8,128)(2,1)}, u32[]{:S(2)}) copy-start(bf16[2,8192,128]{2,1,0:T(8,128)(2,1)} %v_ref.1) | copy-start | bytes 12582916
  5.7 0.9 copy-start.3
  12.0 0.7 copy-start.2
